TPU v7x, 256 devices: a whole 4x4x8 slice. The times are simulated.
256 devices in a mesh: dp: 16 (over x, y), tensor: 16 (over z, core).
Axes of the slice: x: 4, y: 4, z: 8, core: 2. Of those that a mesh axis runs over, the one named last changes fastest.
Arguments:
- hidden: bfloat16 [2048, 16384], P('dp', 'tensor'), may hold values from -6 to 6
- branch: bfloat16 [2048, 16384], P('dp', 'tensor'), may hold values from -6 to 6
- gain: float32 [16384], P('tensor'), may hold values from 0.25 to 1.75
- damping: float32 [16384], P('tensor'), may hold values from 0.5 to 2
Outputs:
- schur: float32 [16384, 16384], P('dp', 'tensor')
- first_panel: float32 [16384, 512], P('dp')
- second_panel: float32 [16384, 512], P('dp')
All inputs are finite; a program needn't handle non-finite values.
Results may differ from a plain program's by a relative error of at most 0.0034.
Values may be sent and summed in bfloat16 or wider, within the bound.
A program may use at most 128 MiB of HBM per device.

v0:
```python
import jax
import jax.numpy as jnp
from jax import lax
from jax.sharding import PartitionSpec as P

D = 16384
PANEL = 512


def spread(block, axis, source):
    block = jnp.where(lax.axis_index(axis) == source, block, jnp.zeros_like(block))
    return lax.psum(block, axis)


def per_device(hidden, branch, gain, damping):
    tok_count = hidden.shape[0]
    width = hidden.shape[1]
    n_rows = lax.axis_size("dp")
    n_cols = lax.axis_size("tensor")
    row_index = lax.axis_index("dp")
    col_index = lax.axis_index("tensor")
    total_tokens = tok_count * n_rows
    row_block = D // n_rows
    summed = hidden.astype(jnp.float32) + branch.astype(jnp.float32)
    squares = lax.psum(jnp.sum(summed * summed, axis=1), "tensor")
    scale = lax.rsqrt(squares / D + 1e-05)
    normed = (summed * scale[:, None] * gain[None, :]).astype(jnp.bfloat16)
    full_rows = lax.all_gather(normed, "tensor", axis=1, tiled=True)
    row_part = lax.all_to_all(full_rows, "dp", split_axis=1, concat_axis=0, tiled=True)
    gram = lax.dot_general(
        row_part,
        lax.all_gather(normed, "dp", axis=0, tiled=True),
        (((0,), (0,)), ((), ())),
        preferred_element_type=jnp.float32,
    )
    rows_global = row_index * row_block + lax.broadcasted_iota(jnp.int32, (row_block, width), 0)
    cols_global = col_index * width + lax.broadcasted_iota(jnp.int32, (row_block, width), 1)
    tile = gram / total_tokens + jnp.where(
        rows_global == cols_global, damping[None, :], jnp.zeros((), jnp.float32)
    )
    panels = []
    for step in range(2):
        offset = step * PANEL
        columns = spread(tile[:, offset : offset + PANEL], "tensor", 0)
        pivot = spread(columns[offset : offset + PANEL], "dp", 0)
        factor = jnp.linalg.cholesky(pivot)
        inverse = lax.linalg.triangular_solve(
            factor, jnp.eye(PANEL, dtype=factor.dtype), left_side=True, lower=True
        )
        own_panel = lax.dot_general(
            columns, inverse, (((1,), (1,)), ((), ())), precision=lax.Precision.HIGHEST
        )
        root = col_index * n_rows // n_cols
        moved = spread(own_panel, "dp", root)
        tile = tile - lax.dot_general(
            own_panel, moved, (((1,), (1,)), ((), ())), precision=lax.Precision.HIGHEST
        )
        panels.append(own_panel)
    return (tile, panels[0], panels[1])


def solution(mesh):
    placed = (P("dp", "tensor"), P("dp", "tensor"), P("tensor"), P("tensor"))
    return jax.shard_map(
        per_device,
        mesh=mesh,
        in_specs=placed,
        out_specs=(P("dp", "tensor"), P("dp", None), P("dp", None)),
        check_vma=False,
    )
```

profile of v0, /device:TPU:99, one launch (start us, length us, event | category | flops | bytes accessed | tf_op | source)
XLA Modules:
  0.0 1165.3 jit_solution(6784582174705465547)
XLA Ops:
  9.6 23.5 %psum.49 = f32[128]{0:T(128)S(1)} all-reduce(f32[128]{0:T(128)S(1)} %multiply_reduce_fusion), channel_id=1, replica_groups=mesh['dp'=16,'tensor'=16] {'tensor'}, use_global_device_ids=true, to_apply=%region_1.0 | all-reduce | flops 128 | bytes 1024 | tf_op jit(solution)/shard_map/psum | solution.py:25
  33.1 1.6 multiply_convert_fusion
  35.5 43.1 %all-gather.3.cloned.1.call-done = bf16[128,16384]{0,1:T(8,128)(2,1)} async-done(((bf16[128,1024]{0,1:T(8,128)(2,1)}), bf16[128,16384]{0,1:T(8,128)(2,1)}) %all-gather.3.cloned.1.call-update) | async-done | bytes 4194320 | tf_op jit(solution)/shard_map/all_gather | solution.py:28
  78.5 6.7 all-to-all-start
  85.3 58.1 %all-to-all-done = bf16[128,16,1024]{0,2,1:T(8,128)(2,1)} async-done(((bf16[128,16,1024]{0,2,1:T(8,128)(2,1)}), bf16[128,16,1024]{0,2,1:T(8,128)(2,1)}, u32[]{:S(2)}, u32[]{:S(2)}) %all-to-all-start) | async-done | bytes 4194336 | tf_op jit(solution)/shard_map/all_to_all | solution.py:29
  143.4 6.4 copy.25
  149.8 32.6 %all-gather.5.cloned.1.call-done = bf16[2048,1024]{0,1:T(8,128)(2,1)} async-done(((bf16[128,1024]{0,1:T(8,128)(2,1)}), bf16[2048,1024]{0,1:T(8,128)(2,1)}) %all-gather.5.cloned.1.call-update) | async-done | bytes 4194320 | tf_op jit(solution)/shard_map/all_gather | solution.py:32
  182.4 7.5 select_add_fusion
  190.0 2.0 copy-done.3
  192.0 1.5 slice_select_fusion.1
  193.6 115.6 %all-reduce.8.cloned.1.call-done = f32[1024,512]{0,1:T(8,128)} async-done(((f32[1024,512]{0,1:T(8,128)}), f32[1024,512]{0,1:T(8,128)}) %all-reduce.8.cloned.1.call-update) | async-done | bytes 2097168 | tf_op jit(solution)/shard_map/psum | solution.py:12
  309.2 2.3 slice_select_fusion.3
  311.8 96.4 %all-reduce.10.cloned.1.call-done = f32[512,512]{0,1:T(8,128)} async-done(((f32[512,512]{0,1:T(8,128)}), f32[512,512]{0,1:T(8,128)}) %all-reduce.10.cloned.1.call-update) | async-done | bytes 1048592 | tf_op jit(solution)/shard_map/psum | solution.py:12
  408.2 1.6 copy.27
  411.1 11.7 %cholesky.286 = f32[128,128]{1,0:T(8,128)S(1)} custom-call(f32[128,128]{1,0:T(8,128)S(1)} %cholesky.426), custom_call_target="Cholesky" | custom-call | tf_op jit(solution)/shard_map/jit(cholesky)/cholesky | solution.py:46
  422.9 9.8 custom-call.27
  432.8 1.2 constant_dynamic-update-slice_fusion.5
  434.0 1.3 convolution_subtract_fusion.9
  435.3 11.7 %cholesky.305 = f32[128,128]{1,0:T(8,128)S(1)} custom-call(f32[128,128]{1,0:T(8,128)S(1)} %cholesky.430), custom_call_target="Cholesky" | custom-call | tf_op jit(solution)/shard_map/jit(cholesky)/cholesky | solution.py:46
  448.4 10.2 custom-call.28
  458.8 1.3 convolution_subtract_fusion.11
  460.1 11.7 %cholesky.326 = f32[128,128]{1,0:T(8,128)S(1)} custom-call(f32[128,128]{1,0:T(8,128)S(1)} %cholesky.435), custom_call_target="Cholesky" | custom-call | tf_op jit(solution)/shard_map/jit(cholesky)/cholesky | solution.py:46
  472.5 9.8 custom-call.29
  483.8 11.7 %cholesky.343 = f32[128,128]{1,0:T(8,128)S(1)} custom-call(f32[128,128]{1,0:T(8,128)S(1)} %convolution_subtract_fusion.13), custom_call_target="Cholesky" | custom-call | tf_op jit(solution)/shard_map/jit(cholesky)/cholesky | solution.py:46
  499.0 7.9 while.4
  499.6 1.4 bitcast_dynamic-update-slice_fusion.4
  501.6 1.4 bitcast_dynamic-update-slice_fusion.4
  503.6 1.4 bitcast_dynamic-update-slice_fusion.4
  505.5 1.4 bitcast_dynamic-update-slice_fusion.4
  506.9 39.3 %custom-call.30 = f32[4,128,128]{1,2,0:T(8,128)S(1)} custom-call(f32[4,128,128]{2,1,0:T(8,128)S(1)} %get-tuple-element.19), custom_call_target="InvertDiagBlocksLowerTriangular" | custom-call | tf_op jit(solution)/shard_map/triangular_solve/custom-call.3 | solution.py:47
  549.4 6.9 fusion
  556.3 2.0 copy.28
  558.3 1.6 broadcast_select_fusion.1
  560.0 100.9 %all-reduce.12.cloned.1.call-done = f32[1024,512]{0,1:T(8,128)} async-done(((f32[1024,512]{0,1:T(8,128)}), f32[1024,512]{0,1:T(8,128)}) %all-reduce.12.cloned.1.call-update) | async-done | bytes 2097168 | tf_op jit(solution)/shard_map/psum | solution.py:12
  660.9 9.6 convolution_subtract_fusion.1
  670.5 2.0 copy-done
  672.5 1.5 slice_select_fusion
  674.1 116.2 %all-reduce.14.cloned.1.call-done = f32[1024,512]{0,1:T(8,128)} async-done(((f32[1024,512]{0,1:T(8,128)}), f32[1024,512]{0,1:T(8,128)}) %all-reduce.14.cloned.1.call-update) | async-done | bytes 2097168 | tf_op jit(solution)/shard_map/psum | solution.py:12
  790.3 2.3 slice_select_fusion.2
  792.7 97.2 %all-reduce.16.cloned.1.call-done = f32[512,512]{0,1:T(8,128)} async-done(((f32[512,512]{0,1:T(8,128)}), f32[512,512]{0,1:T(8,128)}) %all-reduce.16.cloned.1.call-update) | async-done | bytes 1048592 | tf_op jit(solution)/shard_map/psum | solution.py:12
  889.9 1.6 copy.30
  892.7 11.7 %cholesky.358 = f32[128,128]{1,0:T(8,128)S(1)} custom-call(f32[128,128]{1,0:T(8,128)S(1)} %cholesky.439), custom_call_target="Cholesky" | custom-call | tf_op jit(solution)/shard_map/jit(cholesky)/cholesky | solution.py:46
  904.6 9.8 custom-call.31
  914.4 1.2 constant_dynamic-update-slice_fusion.3
  915.7 1.3 convolution_subtract_fusion.8
  917.0 11.7 %cholesky.377 = f32[128,128]{1,0:T(8,128)S(1)} custom-call(f32[128,128]{1,0:T(8,128)S(1)} %cholesky.443), custom_call_target="Cholesky" | custom-call | tf_op jit(solution)/shard_map/jit(cholesky)/cholesky | solution.py:46
  930.0 9.9 custom-call.32
  940.2 1.3 convolution_subtract_fusion.10
  941.6 11.7 %cholesky.398 = f32[128,128]{1,0:T(8,128)S(1)} custom-call(f32[128,128]{1,0:T(8,128)S(1)} %cholesky.448), custom_call_target="Cholesky" | custom-call | tf_op jit(solution)/shard_map/jit(cholesky)/cholesky | solution.py:46
  953.9 9.8 custom-call.33
  964.0 1.2 convolution_subtract_fusion.12
  965.2 11.7 %cholesky.415 = f32[128,128]{1,0:T(8,128)S(1)} custom-call(f32[128,128]{1,0:T(8,128)S(1)} %convolution_subtract_fusion.12), custom_call_target="Cholesky" | custom-call | tf_op jit(solution)/shard_map/jit(cholesky)/cholesky | solution.py:46
  980.4 7.9 while.5
  981.1 1.4 bitcast_dynamic-update-slice_fusion.5
  983.0 1.4 bitcast_dynamic-update-slice_fusion.5
  985.0 1.4 bitcast_dynamic-update-slice_fusion.5
  987.0 1.4 bitcast_dynamic-update-slice_fusion.5
  988.4 39.3 %custom-call.34 = f32[4,128,128]{1,2,0:T(8,128)S(1)} custom-call(f32[4,128,128]{2,1,0:T(8,128)S(1)} %get-tuple-element.20), custom_call_target="InvertDiagBlocksLowerTriangular" | custom-call | tf_op jit(solution)/shard_map/triangular_solve/custom-call.3 | solution.py:47
  1030.9 6.9 fusion.8
  1037.7 2.1 copy.31
  1039.8 1.6 broadcast_select_fusion
  1041.5 100.9 %all-reduce.18.cloned.1.call-done = f32[1024,512]{0,1:T(8,128)} async-done(((f32[1024,512]{0,1:T(8,128)}), f32[1024,512]{0,1:T(8,128)}) %all-reduce.18.cloned.1.call-update) | async-done | bytes 2097168 | tf_op jit(solution)/shard_map/psum | solution.py:12
  1142.4 10.5 convolution_subtract_fusion
  1152.9 5.3 copy.33
  (109 shorter events, 25.8 us)
Async XLA Ops:
  7.2 71.4 %all-gather.3.cloned.1.call-start = ((), (), s32[]{:S(2)}) async-start(), calls=%async_computation.1 | async-start | bytes 4456448 | tf_op jit(solution)/shard_map/all_gather | solution.py:28
  34.7 147.7 %all-gather.5.cloned.1.call-start = ((), (), s32[]{:S(2)}) async-start(), calls=%async_computation.2 | async-start | bytes 4456448 | tf_op jit(solution)/shard_map/all_gather | solution.py:32
  78.5 64.9 %all-to-all-start = ((bf16[128,16,1024]{0,2,1:T(8,128)(2,1)}), bf16[128,16,1024]{0,2,1:T(8,128)(2,1)}, u32[]{:S(2)}, u32[]{:S(2)}) async-start(bf16[128,16,1024]{0,2,1:T(8,128)(2,1)} %bitcast.107), calls=%async_computation | async-start | bytes 8388608 | tf_op jit(solution)/shard_map/all_to_all | solution.py:29
  85.2 223.9 %all-reduce.8.cloned.1.call-start = ((), (), s32[]{:S(2)}) async-start(), calls=%async_computation.3 | async-start | bytes 4194304 | tf_op jit(solution)/shard_map/psum | solution.py:12
  143.4 39.0 %copy-start.10 = (f32[1024]{0:T(1024)S(1)}, f32[1024]{0:T(1024)}, u32[]{:S(2)}) copy-start(f32[1024]{0:T(1024)} %param.10) | copy-start | bytes 12292
  190.0 2.0 copy-start.3
  193.6 214.7 %all-reduce.10.cloned.1.call-start = ((), (), s32[]{:S(2)}) async-start(), calls=%async_computation.4 | async-start | bytes 2097152 | tf_op jit(solution)/shard_map/psum | solution.py:12
  311.5 349.4 %all-reduce.12.cloned.1.call-start = ((), (), s32[]{:S(2)}) async-start(), calls=%async_computation.5 | async-start | bytes 4194304 | tf_op jit(solution)/shard_map/psum | solution.py:12
  408.2 1.7 copy-start.6
  410.1 1.0 copy-start.8
  547.0 2.4 copy-start.4
  556.3 104.6 %copy-start.1 = (f32[1024,512]{1,0:T(8,128)}, f32[1024,512]{1,0:T(8,128)S(1)}, u32[]{:S(2)}) copy-start(f32[1024,512]{1,0:T(8,128)S(1)} %fusion) | copy-start | bytes 6291460
  559.9 230.4 %all-reduce.14.cloned.1.call-start = ((), (), s32[]{:S(2)}) async-start(), calls=%async_computation.6 | async-start | bytes 4194304 | tf_op jit(solution)/shard_map/psum | solution.py:12
  670.5 2.0 copy-start
  674.1 215.8 %all-reduce.16.cloned.1.call-start = ((), (), s32[]{:S(2)}) async-start(), calls=%async_computation.7 | async-start | bytes 2097152 | tf_op jit(solution)/shard_map/psum | solution.py:12
  792.6 349.7 %all-reduce.18.cloned.1.call-start = ((), (), s32[]{:S(2)}) async-start(), calls=%async_computation.8 | async-start | bytes 4194304 | tf_op jit(solution)/shard_map/psum | solution.py:12
  889.9 1.7 copy-start.7
  891.8 1.0 copy-start.9
  1028.5 2.4 copy-start.5
  1037.7 104.6 %copy-start.2 = (f32[1024,512]{1,0:T(8,128)}, f32[1024,512]{1,0:T(8,128)S(1)}, u32[]{:S(2)}) copy-start(f32[1024,512]{1,0:T(8,128)S(1)} %fusion.8) | copy-start | bytes 6291460
Sparse Core Ops, SparseCore 0:
  34.8 43.6 all-gather.2
  81.5 100.8 all-gather.4
  193.7 115.4 all-reduce.7
  312.8 95.3 all-reduce.9
  560.0 100.7 all-reduce.11
  674.2 116.0 all-reduce.13
  794.5 95.3 all-reduce.15
  1041.6 100.7 all-reduce.17
where the time goes:
time: 1170 us
  waiting for transfers between devices  762 us (65%)
  other arithmetic  251 us (21%)
  matrix products  58.5 us (5%)
  local copies, waits for them, and re-layouts  43.2 us (4%)
  blocking collectives  23.5 us (2%)
  between operations  20 us (2%)
    psum x6, waiting for transfers between devices, spread(): return lax.psum(block, axis)  627 us
    another operation x30, other arithmetic, per_device(): factor = jnp.linalg.cholesky(pivot)  159 us
    another operation x5, other arithmetic, per_device(): lax.linalg.triangular_solve(factor, jnp.eye(PANEL, dtype=factor.dtype), l...  79.1 us
    all_to_all x1, waiting for transfers between devices, per_device(): lax.all_to_all(full_rows, 'dp', split_axis=1, concat_axis=0, tiled=True)  58.1 us
    all_gather x1, waiting for transfers between devices, per_device(): full_rows = lax.all_gather(normed, 'tensor', axis=1, tiled=True)  43.1 us
    all_gather x1, waiting for transfers between devices, per_device(): lax.all_gather(normed, 'dp', axis=0, tiled=True)  32.6 us
    psum x1, blocking collectives, per_device(): squares = lax.psum(jnp.sum(summed * summed, axis=1), 'tensor')  23.5 us
  transfers between devices with their start and end apart: 9, of which 9 were waited for; matrix products, arithmetic and copies ran while one was open for 1% of the time, Pallas kernels for 0%

commit v1 on v0

v1 whole, which is shorter than its diff:
```python
import functools

import jax
import jax.numpy as jnp
from jax import lax
from jax.experimental import pallas as pl
from jax.experimental.pallas import tpu as pltpu
from jax.sharding import PartitionSpec as P

D = 16384
TOKENS = 2048
LEAD = 1024
MESH = pl.DeviceIdType.MESH
f32, bf16 = jnp.float32, jnp.bfloat16
NN = (((1,), (0,)), ((), ()))
NT = (((1,), (1,)), ((), ()))
TN = (((0,), (0,)), ((), ()))


def split(x):
    high = x.astype(bf16)
    return high, (x - high.astype(f32)).astype(bf16)


def dot1(x, y, dims):
    return lax.dot_general(x, y, dims, preferred_element_type=f32)


def dot3(x, y, dims):
    (xh, xl), (yh, yl) = split(x), split(y)
    return dot1(xh, yh, dims) + (dot1(xh, yl, dims) + dot1(xl, yh, dims))


def iota(shape, dim):
    return lax.broadcasted_iota(jnp.int32, shape, dim)


def base_inverse(T, b=32, n=128):
    sub, lane = iota((b, n), 0), iota((b, n), 1)
    for o in range(0, n, b):
        R = T[o : o + b, :]
        C = [jnp.broadcast_to(R[:, o + j : o + j + 1], (b, n)) for j in range(b)]
        R = jnp.where((lane >= o) & (lane < o + b), (lane - o == sub).astype(f32), R)
        for j in range(b):
            r = lax.rsqrt(C[j][j : j + 1, :])
            column = jnp.where(sub > j, C[j] * r, 0.0)
            row = R[j : j + 1, :] * r
            R = jnp.where(sub == j, row, R - column * row)
            for m in range(j + 1, b):
                C[m] = C[m] - column * column[m : m + 1, :]
        T[o : o + b, :] = R
        lo = o + b
        if lo < n:
            (Uh, Ul), (Rh, Rl) = split(jnp.where(lane >= lo, R, 0.0)), split(R)
            update = dot1(
                jnp.concatenate([Uh, Uh, Ul], 0), jnp.concatenate([Rh, Rl, Rh], 0), TN
            )
            ln = iota((n - lo, n), 1)
            T[lo:, :] = jnp.where((ln >= o) & (ln < lo), 0.0, T[lo:, :]) - update[lo:, :]
    T[...] = jnp.where(iota((n, n), 0) >= iota((n, n), 1), T[...], 0.0)


def factor(T, block):
    n = LEAD // 128
    for k in range(n):
        rows = slice(k * 128, k * 128 + 128)
        block[...] = T[rows, rows]
        base_inverse(block)
        inverse = block[...]
        if k:
            T[rows, : k * 128] = dot3(inverse, T[rows, : k * 128], NN)
        T[rows, rows] = inverse
        if k < n - 1:
            right = slice(k * 128 + 128, LEAD)
            U = dot3(inverse, T[rows, right], NN)
            T[rows, right] = U
            Uh, Ul = split(U)
            left = T[rows, : k * 128 + 128]
            Lh, Ll = split(left)
            for i in range(k + 1, n):
                at = slice((i - k - 1) * 128, (i - k) * 128)
                own = slice(i * 128, i * 128 + 128)
                uh, ul = Uh[:, at].T, Ul[:, at].T
                low = dot1(uh, Lh, NN) + (dot1(uh, Ll, NN) + dot1(ul, Lh, NN))
                if k:
                    T[own, : k * 128] = T[own, : k * 128] - low[:, : k * 128]
                T[own, rows] = -low[:, k * 128 :]
                rest = slice((i - k - 1) * 128, None)
                T[own, i * 128 :] = T[own, i * 128 :] - (
                    dot1(uh, Uh[:, rest], NN)
                    + (dot1(uh, Ul[:, rest], NN) + dot1(ul, Uh[:, rest], NN))
                )


def compute_body(
    A, B, N0, lead_damping, own_damping, tile, first, second, T, block, lead_t, rows_t, panel, moved_t
):
    on_diagonal = lax.axis_index("dp") == lax.axis_index("tensor")
    step = 256

    def turn(i, _):
        at = pl.ds(pl.multiple_of(i * 128, 128), 128)
        for h in range(2):
            rows = slice(h * 512, h * 512 + 512)
            lead_t[rows, at] = N0[h, at, :].T
            rows_t[rows, at] = B[h, at, :].T
        return 0

    lax.fori_loop(0, TOKENS // 128, turn, 0)

    def lead_gram(i, _):
        at = pl.ds(pl.multiple_of(i * 128, 128), 128)
        lhs = lead_t[at, :]
        for h in range(2):
            T[at, h * 512 : h * 512 + 512] = dot1(lhs, N0[h], NN) * (1.0 / TOKENS)
        return 0

    lax.fori_loop(0, LEAD // 128, lead_gram, 0)
    eye = iota((128, 128), 0) == iota((128, 128), 1)
    for k in range(LEAD // 128):
        at = slice(k * 128, k * 128 + 128)
        T[at, at] = T[at, at] + jnp.where(eye, lead_damping[k : k + 1, :], 0.0)
    factor(T, block)
    n = LEAD // 128
    for k in range(n - 1):
        T[k * 128 : k * 128 + 128, k * 128 + 128 :] = jnp.zeros((128, LEAD - 128 - k * 128), f32)

    dp, tensor = lax.axis_index("dp"), lax.axis_index("tensor")
    for q in range(LEAD // step):
        cols = slice(q * step, q * step + step)
        wide = (q + 1) * step
        weight_h, weight_l = split(T[cols, :wide])

        def own_rows(i, _):
            at = pl.ds(pl.multiple_of(i * step, step), step)
            if q == 0:
                lhs = rows_t[at, :]
                for h in range(2):
                    panel[at, h * 512 : h * 512 + 512] = dot1(lhs, N0[h], NN) * (1.0 / TOKENS)
                rr, cc = iota((step, LEAD), 0), iota((step, LEAD), 1)
                damp = jnp.concatenate([lead_damping[j : j + 1, :] for j in range(8)], 1)
                here = (rr + i * step == cc) & (dp == 0)
                panel[at, :] = panel[at, :] + jnp.where(here, damp, 0.0)
            out = first if q < 2 else second
            sh, sl = split(panel[at, :wide])
            out[at, (q % 2) * step : (q % 2) * step + step] = dot1(sh, weight_h, NT) + (
                dot1(sh, weight_l, NT) + dot1(sl, weight_h, NT)
            )
            return 0

        lax.fori_loop(0, LEAD // step, own_rows, 0)

        def own_cols(i, _):
            at = pl.ds(pl.multiple_of(i * step, step), step)
            if q == 0:
                rhs = A[:, at]
                moved_t[:, at] = dot1(lead_t[...], rhs, NN) * (1.0 / TOKENS)
                damp = jnp.concatenate([lead_damping[j : j + 1, :] for j in range(8)], 1)
                rr, cc = iota((LEAD, step), 0), iota((LEAD, step), 1)
                diag = jnp.concatenate(
                    [
                        jnp.broadcast_to(damp[:, j * 128 : j * 128 + 128].T, (128, step))
                        for j in range(8)
                    ],
                    0,
                )
                here = (cc + i * step == rr) & (tensor == 0)
                moved_t[:, at] = moved_t[:, at] + jnp.where(here, diag, 0.0)
            return 0

        if q == 0:
            lax.fori_loop(0, LEAD // step, own_cols, 0)

    def finish(i, _):
        at = pl.ds(pl.multiple_of(i * step, step), step)
        sh, sl = split(moved_t[:, at])
        parts = []
        for q in range(LEAD // step):
            wide = (q + 1) * step
            wh, wl = split(T[q * step : wide, :wide])
            parts.append(
                dot1(wh, sh[:wide], NN) + (dot1(wh, sl[:wide], NN) + dot1(wl, sh[:wide], NN))
            )
        moved = jnp.concatenate(parts, 0)
        mh, ml = split(moved)
        gram = dot1(rows_t[...], A[:, at], NN) * (1.0 / TOKENS)
        ph, plo = split(first[...])
        qh, qlo = split(second[...])
        half = LEAD // 2
        gram = gram - (dot1(ph, mh[:half], NN) + dot1(qh, mh[half:], NN))
        gram = gram - (dot1(ph, ml[:half], NN) + dot1(qh, ml[half:], NN))
        gram = gram - (dot1(plo, mh[:half], NN) + dot1(qlo, mh[half:], NN))
        tile[:, at] = gram
        return 0

    lax.fori_loop(0, LEAD // step, finish, 0)

    @pl.when(on_diagonal)
    def _():
        for k in range(n):
            at = slice(k * 128, k * 128 + 128)
            tile[at, at] = tile[at, at] + jnp.where(eye, own_damping[k : k + 1, :], 0.0)


def compute(A, B, N0, lead_damping, own_damping):
    vm = pl.BlockSpec(memory_space=pltpu.VMEM)
    return pl.pallas_call(
        compute_body,
        out_shape=(
            jax.ShapeDtypeStruct((LEAD, LEAD), f32),
            jax.ShapeDtypeStruct((LEAD, LEAD // 2), f32),
            jax.ShapeDtypeStruct((LEAD, LEAD // 2), f32),
        ),
        in_specs=[vm] * 5,
        out_specs=(vm,) * 3,
        scratch_shapes=[
            pltpu.VMEM((LEAD, LEAD), f32),
            pltpu.VMEM((128, 128), f32),
            pltpu.VMEM((LEAD, TOKENS), bf16),
            pltpu.VMEM((LEAD, TOKENS), bf16),
            pltpu.VMEM((LEAD, LEAD), f32),
            pltpu.VMEM((LEAD, LEAD), f32),
        ],
        compiler_params=pltpu.CompilerParams(vmem_limit_bytes=60 * 2**20),
    )(A, B, N0, lead_damping, own_damping)


def strip_of(kind, k, x, y):
    if kind == 0:
        return (slice(None), lax.rem(y + k, 4), pl.ds(0, 64))
    return (lax.rem(x + k, 4), slice(None), pl.ds(64, 64))


def gather_body(
    hidden, branch, gain, damping, A, B, N0, lead_damping,
    parts, n_sem, part_send, part_recv, z_send, z_recv, sib_send, sib_recv,
    g_send, g_recv, x_send, x_recv, b_send, b_recv, e_send, e_recv, local_sem,
):
    d, t = lax.axis_index("dp"), lax.axis_index("tensor")
    x, y, z, c = d // 4, d % 4, t // 2, t % 2
    sibling = (d, t + 1 - 2 * c)
    along = {
        (0, 1): (lax.rem(x + 1, 4) * 4 + y, t),
        (0, -1): (lax.rem(x + 3, 4) * 4 + y, t),
        (1, 1): (x * 4 + lax.rem(y + 1, 4), t),
        (1, -1): (x * 4 + lax.rem(y + 3, 4), t),
    }
    up = (d, lax.rem(z + 1, 8) * 2 + c)
    down = (d, lax.rem(z + 7, 8) * 2 + c)
    same = [(d, lax.rem(t + i, 16)) for i in range(1, 16)]

    barrier = pltpu.get_barrier_semaphore()
    partners = same + list(along.values())
    for partner in partners:
        pl.semaphore_signal(barrier, inc=1, device_id=partner, device_id_type=MESH)

    def remote(src, dst, send, recv, to):
        return pltpu.make_async_remote_copy(
            src_ref=src, dst_ref=dst, send_sem=send, recv_sem=recv, device_id=to, device_id_type=MESH
        )

    total = hidden[...].astype(f32) + branch[...].astype(f32)
    own = jnp.broadcast_to(jnp.sum(total * total, axis=1, keepdims=True), (128, 128))
    parts[0, 0:8, :] = own.T[0:8, :]
    parts[0, 8:16, :] = damping[...]
    pl.semaphore_wait(barrier, len(partners))
    part_copies = [
        remote(parts.at[0], parts.at[i], part_send.at[i], part_recv.at[i], same[i - 1])
        for i in range(1, 16)
    ]
    for copy in part_copies:
        copy.start()
    for copy in part_copies:
        copy.wait_recv()
    squares = parts[0, 0:1, :]
    for i in range(1, 16):
        squares = squares + parts[i, 0:1, :]
    lead_damping[...] = parts[t, 8:16, :]
    scale = lax.rsqrt(squares / D + 1e-05)
    column = jnp.broadcast_to(scale, (128, 128)).T
    for j in range(8):
        at = slice(j * 128, j * 128 + 128)
        block = hidden[:, at].astype(f32) + branch[:, at].astype(f32)
        A[x, y, :, at] = (block * column * gain[j : j + 1, :]).astype(bf16)

    def both_ways(ref, which):
        copies = {}
        for kind in range(2):
            at = (x, y, pl.ds(64 * kind, 64))
            for side, s in ((1, 0), (-1, 1)):
                copies[kind, side] = remote(
                    ref.at[at], ref.at[at], g_send.at[which, 0, kind, s], g_recv.at[which, 0, kind, s],
                    along[kind, side],
                )
        return copies

    def pass_on(ref, which):
        copies = {}
        for kind in range(2):
            for side, s in ((1, 0), (-1, 1)):
                back = 4 - side
                at = (lax.rem(x + back, 4), y) if kind == 0 else (x, lax.rem(y + back, 4))
                at = at + (pl.ds(64 * kind + 32 * s, 32),)
                copies[kind, side] = remote(
                    ref.at[at], ref.at[at], g_send.at[which, 1, kind, s], g_recv.at[which, 1, kind, s],
                    along[kind, side],
                )
        return copies

    def strips(ref, which):
        copies = {}
        for kind in range(2):
            at = strip_of(kind, 0, x, y)
            for side, s in ((1, 0), (-1, 1)):
                copies[kind, side] = remote(
                    ref.at[at], ref.at[at], g_send.at[which, 2, kind, s], g_recv.at[which, 2, kind, s],
                    along[1 - kind, side],
                )
        return copies

    def strips_on(ref, which):
        copies = {}
        for kind in range(2):
            for side, s in ((1, 0), (-1, 1)):
                at = strip_of(kind, 4 - side, x, y)
                at = at[:2] + (pl.ds(64 * kind + 32 * s, 32),)
                copies[kind, side] = remote(
                    ref.at[at], ref.at[at], g_send.at[which, 3, kind, s], g_recv.at[which, 3, kind, s],
                    along[1 - kind, side],
                )
        return copies

    def start(copies):
        for copy in copies.values():
            copy.start()
        return copies

    def arrive(copies):
        for copy in copies.values():
            copy.wait_recv()

    def sent(copies):
        for copy in copies.values():
            copy.wait_send()

    a_first = start(both_ways(A, 0))

    half = N0.at[c]
    chunks = [pl.ds(32 * q, 32) for q in range(4)]
    source = (x, y)

    @pl.when(t == 0)
    def _():
        for q in range(4):
            remote(
                A.at[x, y, chunks[q], pl.ds(512, 512)], N0.at[1, x, y, chunks[q]],
                sib_send.at[q], z_recv.at[q], sibling,
            ).start()
        N0[0, x, y] = A[x, y, :, 0:512]

    rising, falling = [], []
    for q in range(4):
        at = half.at[source + (chunks[q],)]
        rising.append(remote(at, at, z_send.at[0, q], z_recv.at[q], up))
        falling.append(remote(at, at, z_send.at[1, q], z_recv.at[q], down))

        @pl.when(t != 0)
        def _():
            rising[q].wait_recv()

        @pl.when(z < 4)
        def _():
            rising[q].start()

        @pl.when((z == 0) | (z > 5))
        def _():
            falling[q].start()

    n_first = start(both_ways(half, 1))
    arrive(a_first)
    a_second = start(pass_on(A, 0))
    arrive(n_first)
    n_second = start(pass_on(half, 1))

    def give(kind, k):
        at = (c,) + strip_of(kind, k, x, y)
        copy = remote(N0.at[at], N0.at[at], x_send.at[kind, k], x_recv.at[kind, k], sibling)
        copy.start()
        return copy

    gifts = []
    arrive(n_second)
    n_third = start(strips(half, 1))
    gifts += [give(kind, 0) for kind in range(2)]
    arrive(a_second)
    a_third = start(strips(A, 0))

    origin = d // 2
    rise = lax.rem(z - origin + 8, 8)
    at_origin = rise == 0
    is_source = t == d

    def piece(kind, k, j):
        if kind == 0:
            return (j, lax.rem(y + k, 4), pl.ds(0, 64))
        return (lax.rem(x + k, 4), j, pl.ds(64, 64))

    order = {0: 0, 1: 1, 3: 2, 2: 3}

    def b_from_source(k):
        @pl.when(is_source)
        def _():
            for kind in range(2):
                at = strip_of(kind, k, x, y)
                n = order[k]
                for j in range(4):
                    sub = piece(kind, k, j)
                    remote(
                        A.at[sub + (pl.ds(pl.multiple_of(c * 512, 512), 512),)], B.at[(c,) + sub],
                        b_send.at[kind, n, j], b_recv.at[kind, n, j], up if kind == 0 else down,
                    ).start()
                    remote(
                        A.at[sub + (pl.ds(pl.multiple_of(512 - c * 512, 512), 512),)], B.at[(1 - c,) + sub],
                        e_send.at[kind, n, 1 + j], b_recv.at[kind, n, j], sibling,
                    ).start()
                remote(
                    A.at[at + (pl.ds(pl.multiple_of(c * 512, 512), 512),)], B.at[(c,) + at],
                    e_send.at[kind, n, 0], e_recv.at[kind, n], sibling,
                ).start()
                for h in range(2):
                    pltpu.make_async_copy(
                        A.at[at + (pl.ds(512 * h, 512),)], B.at[(h,) + at], local_sem.at[kind, n, h]
                    ).start()

    def b_relay(k):
        n = order[k]
        for j in range(4):
            for kind in range(2):
                sub = (c,) + piece(kind, k, j)
                on = remote(
                    B.at[sub], B.at[sub], b_send.at[kind, n, j], b_recv.at[kind, n, j],
                    up if kind == 0 else down,
                )
                last = rise == (7 if kind == 0 else 1)

                @pl.when(jnp.logical_not(is_source))
                def _():
                    on.wait_recv()

                @pl.when(jnp.logical_not(is_source | last))
                def _():
                    on.start()

        @pl.when(jnp.logical_not(at_origin))
        def _():
            for kind in range(2):
                at = (c,) + strip_of(kind, k, x, y)
                remote(B.at[at], B.at[at], e_send.at[kind, n, 0], e_recv.at[kind, n], sibling).start()

    def b_end(k):
        n = order[k]
        for kind in range(2):
            at = strip_of(kind, k, x, y)
            whole = (c,) + at
            swap = remote(B.at[whole], B.at[whole], e_send.at[kind, n, 0], e_recv.at[kind, n], sibling)
            last = rise == (7 if kind == 0 else 1)

            @pl.when(jnp.logical_not(is_source))
            def _():
                swap.wait_recv()

            @pl.when(jnp.logical_not(at_origin) | is_source)
            def _():
                swap.wait_send()

            for j in range(4):
                sub = (c,) + piece(kind, k, j)
                on = remote(
                    B.at[sub], B.at[sub], b_send.at[kind, n, j], b_recv.at[kind, n, j],
                    up if kind == 0 else down,
                )

                @pl.when(jnp.logical_not(last))
                def _():
                    on.wait_send()

                @pl.when(is_source)
                def _():
                    remote(
                        B.at[sub], B.at[sub], e_send.at[kind, n, 1 + j], b_recv.at[kind, n, j], sibling
                    ).wait_send()

            @pl.when(is_source)
            def _():
                for h in range(2):
                    pltpu.make_async_copy(
                        A.at[at + (pl.ds(512 * h, 512),)], B.at[(h,) + at], local_sem.at[kind, n, h]
                    ).wait()

    b_from_source(0)
    arrive(n_third)
    n_fourth = start(strips_on(half, 1))
    gifts += [give(kind, k) for k in (1, 3) for kind in range(2)]
    arrive(n_fourth)
    gifts += [give(kind, 2) for kind in range(2)]
    b_relay(0)
    arrive(a_third)
    a_fourth = start(strips_on(A, 0))
    b_from_source(1)
    b_from_source(3)
    arrive(a_fourth)
    b_from_source(2)
    for k in (1, 3, 2):
        b_relay(k)
    for copy in gifts:
        copy.wait()
    for k in (0, 1, 3, 2):
        b_end(k)
    for copies in (a_first, a_second, a_third, a_fourth, n_first, n_second, n_third, n_fourth):
        sent(copies)
    for copy in part_copies:
        copy.wait_send()
    for q in range(4):

        @pl.when(t == 0)
        def _():
            remote(
                A.at[x, y, chunks[q], pl.ds(512, 512)], N0.at[1, x, y, chunks[q]],
                sib_send.at[q], z_recv.at[q], sibling,
            ).wait_send()

        @pl.when(z < 4)
        def _():
            rising[q].wait_send()

        @pl.when((z == 0) | (z > 5))
        def _():
            falling[q].wait_send()


def gather(hidden, branch, gain, damping):
    vm = pl.BlockSpec(memory_space=pltpu.VMEM)
    dma = pltpu.SemaphoreType.DMA
    return pl.pallas_call(
        gather_body,
        out_shape=(
            jax.ShapeDtypeStruct((4, 4, 128, LEAD), bf16),
            jax.ShapeDtypeStruct((2, 4, 4, 128, LEAD // 2), bf16),
            jax.ShapeDtypeStruct((2, 4, 4, 128, LEAD // 2), bf16),
            jax.ShapeDtypeStruct((8, 128), f32),
        ),
        in_specs=[vm] * 4,
        out_specs=(vm,) * 4,
        scratch_shapes=[
            pltpu.VMEM((16, 16, 128), f32),
            dma((1,)),
            dma((16,)),
            dma((16,)),
            dma((2, 4)),
            dma((4,)),
            dma((4,)),
            dma((4,)),
            dma((2, 4, 2, 2)),
            dma((2, 4, 2, 2)),
            dma((2, 4)),
            dma((2, 4)),
            dma((2, 4, 4)),
            dma((2, 4, 4)),
            dma((2, 4, 5)),
            dma((2, 4)),
            dma((2, 4, 2)),
        ],
        compiler_params=pltpu.CompilerParams(
            collective_id=0, has_side_effects=True, vmem_limit_bytes=40 * 2**20
        ),
    )(hidden, branch, gain, damping)


def per_device(hidden, branch, gain, damping):
    gain, damping = gain.reshape(8, 128), damping.reshape(8, 128)
    A, B, N0, lead_damping = gather(hidden, branch, gain, damping)
    A = A.reshape(TOKENS, LEAD)
    B, N0 = B.reshape(2, TOKENS, LEAD // 2), N0.reshape(2, TOKENS, LEAD // 2)
    return compute(A, B, N0, lead_damping, damping)


def solution(mesh):
    return jax.shard_map(
        per_device,
        mesh=mesh,
        in_specs=(P("dp", "tensor"), P("dp", "tensor"), P("tensor"), P("tensor")),
        out_specs=(P("dp", "tensor"), P("dp", None), P("dp", None)),
        check_vma=False,
    )
```

time: 1170 us -> 817 us (0.70)
  Pallas kernels: 0 us -> 806 us
  waiting for transfers between devices: 762 us -> 0 us
  other arithmetic: 251 us -> 0 us
  matrix products: 58.5 us -> 0 us
  local copies, waits for them, and re-layouts: 43.2 us -> 9.72 us
  blocking collectives: 23.5 us -> 0 us
  between operations: 20 us -> 0.66 us
    pallas_call x0 -> x2, Pallas kernels: none -> 806 us  [the longest x1 727 us: gather(): pl.pallas_call(gather_body, out_shape=(jax.ShapeDtypeStruct((4, 4, 128, L...]
    psum x6 -> x0, waiting for transfers between devices: 627 us -> none  [spread(): return lax.psum(block, axis)]
    another operation x35 -> x0, other arithmetic: 238 us -> none  [the longest x30 159 us: per_device(): factor = jnp.linalg.cholesky(pivot)]
    all_gather x2 -> x0, waiting for transfers between devices: 75.6 us -> none  [the longest x1 43.1 us: per_device(): full_rows = lax.all_gather(normed, 'tensor', axis=1, tiled=True)]
    all_to_all x1 -> x0, waiting for transfers between devices: 58.1 us -> none  [per_device(): lax.all_to_all(full_rows, 'dp', split_axis=1, concat_axis=0, tiled=True)]
    dot_general x5 -> x0, matrix products: 41.4 us -> none  [the longest x2 20.1 us: per_device(): lax.dot_general(own_panel, moved, (((1,), (1,)), ((), ())), precision=lax...]
    psum x1 -> x0, blocking collectives: 23.5 us -> none  [per_device(): squares = lax.psum(jnp.sum(summed * summed, axis=1), 'tensor')]
    another operation x26 -> x0, matrix products: 17.1 us -> none  [the longest x12 10.9 us: per_device(): factor = jnp.linalg.cholesky(pivot)]
  transfers between devices with their start and end apart: 9 -> 0, of which waited for: 9 -> 0; matrix products, arithmetic and copies ran while one was open for 1% -> 0% of each run, Pallas kernels for 0% -> 0%
where the time goes in v1:
time: 817 us; the launch traced here: 816 us
  Pallas kernels  806 us (99%)
  local copies, waits for them, and re-layouts  9.72 us (1%)
    pallas_call x1, Pallas kernels, gather(): pl.pallas_call(gather_body, out_shape=(jax.ShapeDtypeStruct((4, 4, 128, L...  727 us
    pallas_call x1, Pallas kernels, compute(): pl.pallas_call(compute_body, out_shape=(jax.ShapeDtypeStruct((LEAD, LEAD)...  78.7 us

profile of v1, /device:TPU:99, one launch (start us, length us, event | category | flops | bytes accessed | tf_op | source)
XLA Modules:
  0.0 816.4 jit_solution(16318424537232164058)
XLA Ops:
  0.6 0.0 copy-start.3
  0.6 0.9 copy-done.3
  1.6 0.0 copy-start.4
  1.6 0.9 copy-done.4
  2.5 0.0 copy-start.5
  2.5 0.7 copy-done.5
  3.2 0.0 copy-start.6
  3.2 0.7 copy-done.6
  3.9 727.2 %shard_map.67 = (bf16[4,4,128,1024]{3,2,1,0:T(8,128)(2,1)S(1)}, bf16[2,4,4,128,512]{4,3,2,1,0:T(8,128)(2,1)S(1)}, bf16[2,4,4,128,512]{4,3,2,1,0:T(8,128)(2,1)S(1)}, f32[8,128]{1,0:T(8,128)S(1)}) custom-call(bf16[128,1024]{1,0:T(8,128)(2,1)S(1)} %copy-done.3, bf16[128,1024]{1,0:T(8,128)(2,1)S(1)} %copy-done.4, f32[8,128]{1,0:T(8,128)S(1)} %bitcast.10, ...), custom_call_target="tpu_custom_call" | custom-call | tf_op jit(solution)/shard_map/pallas_call | solution.py:544
  731.2 0.0 copy-start
  731.2 1.9 copy-done
  733.1 0.0 copy-start.1
  733.1 2.0 copy-done.1
  735.1 0.0 copy-start.2
  735.1 2.0 copy-done.2
  737.0 0.0 copy-start.7
  737.0 0.6 copy-done.7
  737.6 78.7 %shard_map.68 = (f32[1024,1024]{1,0:T(8,128)}, f32[1024,512]{1,0:T(8,128)}, f32[1024,512]{1,0:T(8,128)}) custom-call(bf16[2048,1024]{1,0:T(8,128)(2,1)} %bitcast.5, bf16[2,2048,512]{2,1,0:T(8,128)(2,1)} %bitcast.6, bf16[2,2048,512]{2,1,0:T(8,128)(2,1)} %bitcast.7, f32[8,128]{1,0:T(8,128)} %copy-done.7, f32[8,128]{1,0:T(8,128)} %bitcast.8), custom_call_target="tpu_custom_call" | custom-call | tf_op jit(solution)/shard_map/pallas_call | solution.py:207
Async XLA Ops:
  0.6 1.0 copy-start.3
  1.6 0.9 copy-start.4
  2.5 0.7 copy-start.5
  3.2 0.7 copy-start.6
  731.2 1.9 copy-start
  733.1 2.0 copy-start.1
  735.1 2.0 copy-start.2
  737.0 0.6 copy-start.7
